TPU v7x, 256 devices: a whole 4x4x8 slice. The times are simulated.
256 devices in a mesh: row: 4 (over z_lo, core), col: 16 (over x, y), chan: 4 (over z_hi).
Axes of the slice: x: 4, y: 4, z: 8 (z_hi: 4, z_lo: 2; z = z_hi * 2 + z_lo), core: 2. Of those that a mesh axis runs over, the one named last changes fastest.
Arguments:
- pair: bfloat16 [1024, 1024, 128], P('row', 'col'), may hold values from -6 to 6
- pair_mask: int32 [1024, 1024], P('row', 'col'), may hold values 0 or 1
- ln_gain: float32 [128], replicated, may hold values from 0.1 to 1.9
- ln_bias: float32 [128], replicated, may hold values from -3 to 3
- left_value: bfloat16 [128, 128], P(None, 'chan'), may hold values from -0.5 to 0.5
- left_gate: bfloat16 [128, 128], P(None, 'chan'), may hold values from -0.5 to 0.5
- right_value: bfloat16 [128, 128], P(None, 'chan'), may hold values from -0.5 to 0.5
- right_gate: bfloat16 [128, 128], P(None, 'chan'), may hold values from -0.5 to 0.5
- hid_gain: float32 [128], replicated, may hold values from 0.1 to 1.9
- hid_bias: float32 [128], replicated, may hold values from -3 to 3
- out_weight: bfloat16 [128, 128], replicated, may hold values from -0.5 to 0.5
- out_gate: bfloat16 [128, 128], replicated, may hold values from -0.5 to 0.5
Outputs:
- update: bfloat16 [1024, 1024, 128], P('row', ('col', 'chan'))
All inputs are finite; a program needn't handle non-finite values. No bound on the sum of `pair_mask` on one device may be relied on, other than what follows from the above.
Results may differ from a plain program's by a relative error of at most 0.025.
Values may be sent and summed in bfloat16 or wider, within the bound.
No kernel may reach another device: no remote copies, remote signals or barrier semaphores. Data moves between devices by JAX's collectives and lax.ppermute only.
A program may use at most 128 MiB of HBM per device.

v0:
```python
import jax
import jax.numpy as jnp
from jax import lax
from jax.sharding import PartitionSpec as P


def on_device(
    pair,
    pair_mask,
    ln_gain,
    ln_bias,
    left_value,
    left_gate,
    right_value,
    right_gate,
    hid_gain,
    hid_bias,
    out_weight,
    out_gate,
):
    tile_cols = pair.shape[1]
    group_width = left_value.shape[1]
    out_cols = tile_cols // lax.axis_size("chan")
    group_index = lax.axis_index("chan")
    source = pair.astype(jnp.float32)
    centre = jnp.mean(source, axis=-1, keepdims=True)
    shifted = source - centre
    spread = jnp.mean(shifted * shifted, axis=-1, keepdims=True)
    normed = (shifted * lax.rsqrt(spread + 1e-05) * ln_gain + ln_bias).astype(jnp.bfloat16)
    weights = jnp.concatenate([left_value, left_gate, right_value, right_gate], axis=1)
    projected_all = jnp.einsum("ikc,cq->qik", normed, weights, preferred_element_type=jnp.float32)
    valid = pair_mask.astype(jnp.float32)[None, :, :]
    left = (
        jax.nn.sigmoid(projected_all[group_width : 2 * group_width])
        * projected_all[:group_width]
        * valid
    ).astype(jnp.bfloat16)
    right = (
        jax.nn.sigmoid(projected_all[3 * group_width :])
        * projected_all[2 * group_width : 3 * group_width]
        * valid
    ).astype(jnp.bfloat16)
    own_normed = lax.dynamic_slice_in_dim(normed, group_index * out_cols, out_cols, 1)
    gating = jax.nn.sigmoid(
        jnp.einsum("ijc,cd->ijd", own_normed, out_gate, preferred_element_type=jnp.float32)
    )
    right_all = lax.all_gather(right, "row", axis=1, tiled=True)
    product = lax.psum_scatter(
        jnp.einsum("hik,hjk->jhi", left, right_all, preferred_element_type=jnp.float32).astype(
            jnp.bfloat16
        ),
        "col",
        scatter_dimension=0,
        tiled=True,
    ).astype(jnp.float32)
    product = product.astype(jnp.bfloat16)
    widened = product.astype(jnp.float32)
    first_sums = jnp.sum(widened, axis=1)
    second_sums = jnp.sum(widened * widened, axis=1)
    first_sums, second_sums = (
        lax.psum(first_sums.astype(jnp.bfloat16), "chan").astype(jnp.float32),
        lax.psum(second_sums.astype(jnp.bfloat16), "chan").astype(jnp.float32),
    )
    total_width = group_width * lax.axis_size("chan")
    mean_hid = first_sums / total_width
    spread_hid = second_sums / total_width - mean_hid * mean_hid
    gain_part = lax.dynamic_slice_in_dim(hid_gain, group_index * group_width, group_width, 0)
    bias_part = lax.dynamic_slice_in_dim(hid_bias, group_index * group_width, group_width, 0)
    weight_rows = lax.dynamic_slice_in_dim(out_weight, group_index * group_width, group_width, 0)
    hidden = (
        (widened - mean_hid[:, None, :])
        * lax.rsqrt(spread_hid + 1e-05)[:, None, :]
        * gain_part[None, :, None]
        + bias_part[None, :, None]
    ).astype(jnp.bfloat16)
    mixed = lax.psum_scatter(
        jnp.einsum("jhi,hd->jid", hidden, weight_rows, preferred_element_type=jnp.float32).astype(
            jnp.bfloat16
        ),
        "chan",
        scatter_dimension=0,
        tiled=True,
    ).astype(jnp.float32)
    return (gating * jnp.transpose(mixed, (1, 0, 2))).astype(jnp.bfloat16)


def solution(mesh):
    return jax.shard_map(
        on_device,
        mesh=mesh,
        in_specs=(
            P("row", "col", None),
            P("row", "col"),
            P(),
            P(),
            P(None, "chan"),
            P(None, "chan"),
            P(None, "chan"),
            P(None, "chan"),
            P(),
            P(),
            P(),
            P(),
        ),
        out_specs=P("row", ("col", "chan"), None),
        check_vma=False,
    )
```

profile of v0, /device:TPU:1, one launch (start us, length us, event | category | flops | bytes accessed | tf_op | source)
XLA Modules:
  0.0 375.0 jit_solution(5184248092818221821)
XLA Ops:
  6.5 0.0 all-gather.2.cloned.1.call-start
  6.6 10.7 %convert_reduce_fusion = f32[256,64]{0,1:T(8,128)S(1)} fusion(bf16[256,64,128]{2,1,0:T(8,128)(2,1)} %param.12), kind=kLoop, calls=%fused_computation.2 | loop fusion | flops 4177920 | bytes 4259840 | tf_op jit(solution)/shard_map/reduce_sum | solution.py:26
  17.3 11.6 %fusion.2 = f32[256,64]{0,1:T(8,128)S(1)} fusion(f32[256,64]{0,1:T(8,128)S(1)} %broadcast_multiply_fusion, bf16[256,64,128]{2,1,0:T(8,128)(2,1)S(1)} %copy-done.1), kind=kLoop, calls=%fused_computation.5 | loop fusion | flops 8372224 | bytes 4325376 | tf_op jit(solution)/shard_map/reduce_sum | solution.py:28
  29.0 0.0 copy-start.4
  29.0 0.0 copy-start.5
  29.0 0.0 copy-start.6
  29.1 9.3 %fusion.5 = bf16[256,64,128]{2,0,1:T(8,128)(2,1)S(1)} fusion(f32[128]{0:T(128)S(1)} %copy-done.8, f32[128]{0:T(128)S(1)} %copy-done.9, f32[256,64]{0,1:T(8,128)S(1)} %add_rsqrt_fusion.1, f32[256,64]{0,1:T(8,128)S(1)} %broadcast_multiply_fusion, bf16[256,64,128]{2,1,0:T(8,128)(2,1)S(1)} %copy-done.1), kind=kLoop, calls=%fused_computation.8 | loop fusion | flops 12582912 | bytes 8520704 | tf_op jit(solution)/shard_map/convert_element_type | solution.py:29
  38.4 1.3 fusion.26
  39.7 0.7 copy-done.2
  40.3 2.4 fusion.13
  42.7 0.0 all-gather.2.cloned.1.call-update
  42.8 0.0 reduce-scatter.3.cloned.1.call-start
  42.8 53.4 %all-gather.2.cloned.1.call-done = bf16[32,1024,64]{1,0,2:T(8,128)(2,1)} async-done(((bf16[32,256,64]{1,0,2:T(8,128)(2,1)}), bf16[32,1024,64]{1,0,2:T(8,128)(2,1)}) %all-gather.2.cloned.1.call-update) | async-done | bytes 4194320 | tf_op jit(solution)/shard_map/all_gather | solution.py:47
  96.2 10.3 %convert_bitcast_fusion = bf16[1024,32,256]{2,0,1:T(8,128)(2,1)} fusion(bf16[32,1024,64]{1,0,2:T(8,128)(2,1)} %all-gather.2.cloned.1.call-done, bf16[32,256,64]{1,0,2:T(8,128)(2,1)S(1)} %get-tuple-element.7), kind=kOutput, calls=%fused_computation | convolution fusion | flops 1082130432 | bytes 22020096 | tf_op jit(solution)/shard_map/hik,hjk->jhi/dot_general | solution.py:49
  106.5 0.0 reduce-scatter.3.cloned.1.call-update
  106.5 0.0 all-reduce.3.cloned.1.call-start
  106.6 115.2 %reduce-scatter.3.cloned.1.call-done = bf16[64,32,256]{2,0,1:T(8,128)(2,1)} async-done(((bf16[1024,32,256]{2,0,1:T(8,128)(2,1)}), bf16[64,32,256]{2,0,1:T(8,128)(2,1)}) %reduce-scatter.3.cloned.1.call-update) | async-done | bytes 1048592 | tf_op jit(solution)/shard_map/reduce_scatter | solution.py:48
  221.8 2.1 fusion.11
  223.8 2.0 reduce_sum.41
  225.8 0.0 all-reduce.3.cloned.1.call-update
  225.8 0.3 reduce-scatter.5.cloned.1.call-start
  226.1 0.1 dynamic_slice.13
  226.2 0.1 dynamic_slice.14
  226.3 47.2 %all-reduce.3.cloned.1.call-done = (bf16[64,256]{1,0:T(8,128)(2,1)}, bf16[64,256]{1,0:T(8,128)(2,1)}) async-done(((bf16[64,256]{1,0:T(8,128)(2,1)}, bf16[64,256]{1,0:T(8,128)(2,1)}), (bf16[64,256]{1,0:T(8,128)(2,1)}, bf16[64,256]{1,0:T(8,128)(2,1)})) %all-reduce.3.cloned.1.call-update) | async-done | bytes 65552 | tf_op jit(solution)/shard_map/psum | solution.py:62
  273.5 0.8 convert_multiply_fusion.1
  274.3 1.6 fusion.10
  275.9 0.0 copy-start.10
  275.9 3.3 convolution_convert_fusion
  279.2 0.0 reduce-scatter.5.cloned.1.call-update
  279.2 85.3 %reduce-scatter.5.cloned.1.call-done = bf16[16,256,128]{2,1,0:T(8,128)(2,1)} async-done(((bf16[64,256,128]{2,1,0:T(8,128)(2,1)}), bf16[16,256,128]{2,1,0:T(8,128)(2,1)}) %reduce-scatter.5.cloned.1.call-update) | async-done | bytes 1048592 | tf_op jit(solution)/shard_map/reduce_scatter | solution.py:76
  364.5 2.2 fusion.22
  366.8 1.6 copy.17
  (24 shorter events, 0.1 us)
Async XLA Ops:
  6.5 269.4 %copy-start = (bf16[128,128]{1,0:T(8,128)(2,1)S(1)}, bf16[128,128]{1,0:T(8,128)(2,1)}, u32[]{:S(2)}) copy-start(bf16[128,128]{1,0:T(8,128)(2,1)} %param.22) | copy-start | bytes 98308
  6.5 22.4 %copy-start.3 = (s32[256,64]{0,1:T(8,128)S(1)}, s32[256,64]{0,1:T(8,128)}, u32[]{:S(2)}) copy-start(s32[256,64]{0,1:T(8,128)} %param.13) | copy-start | bytes 196612
  6.5 22.5 %copy-start.9 = (f32[128]{0:T(128)S(1)}, f32[128]{0:T(128)}, u32[]{:S(2)}) copy-start(f32[128]{0:T(128)} %param.14) | copy-start | bytes 1540
  6.5 22.5 %copy-start.8 = (f32[128]{0:T(128)S(1)}, f32[128]{0:T(128)}, u32[]{:S(2)}) copy-start(f32[128]{0:T(128)} %param.15) | copy-start | bytes 1540
  6.5 89.7 %all-gather.2.cloned.1.call-start = ((), (), s32[]{:S(2)}) async-start(), calls=%async_computation.2 | async-start | bytes 5242880 | tf_op jit(solution)/shard_map/all_gather | solution.py:47
  6.6 10.7 %copy-start.1 = (bf16[256,64,128]{2,1,0:T(8,128)(2,1)S(1)}, bf16[256,64,128]{2,1,0:T(8,128)(2,1)}, u32[]{:S(2)}) copy-start(bf16[256,64,128]{2,1,0:T(8,128)(2,1)} %param.12) | copy-start | bytes 12582916
  29.0 9.3 %copy-start.4 = (bf16[128,32]{0,1:T(8,128)(2,1)S(1)}, bf16[128,32]{0,1:T(8,128)(2,1)}, u32[]{:S(2)}) copy-start(bf16[128,32]{0,1:T(8,128)(2,1)} %param.19) | copy-start | bytes 24580
  29.0 9.3 %copy-start.5 = (bf16[128,32]{0,1:T(8,128)(2,1)S(1)}, bf16[128,32]{0,1:T(8,128)(2,1)}, u32[]{:S(2)}) copy-start(bf16[128,32]{0,1:T(8,128)(2,1)} %param.18) | copy-start | bytes 24580
  29.0 9.3 %copy-start.6 = (bf16[128,32]{0,1:T(8,128)(2,1)S(1)}, bf16[128,32]{0,1:T(8,128)(2,1)}, u32[]{:S(2)}) copy-start(bf16[128,32]{0,1:T(8,128)(2,1)} %param.17) | copy-start | bytes 24580
  29.1 9.3 %copy-start.7 = (bf16[128,32]{0,1:T(8,128)(2,1)S(1)}, bf16[128,32]{0,1:T(8,128)(2,1)}, u32[]{:S(2)}) copy-start(bf16[128,32]{0,1:T(8,128)(2,1)} %param.16) | copy-start | bytes 24580
  38.4 1.9 copy-start.2
  42.8 179.0 %reduce-scatter.3.cloned.1.call-start = ((), (), s32[]{:S(2)}) async-start(), calls=%async_computation.3 | async-start | bytes 17825792 | tf_op jit(solution)/shard_map/reduce_scatter | solution.py:48
  106.5 119.6 %copy-start.11 = (f32[128]{0:T(128)S(1)}, f32[128]{0:T(128)}, u32[]{:S(2)}) copy-start(f32[128]{0:T(128)} %param.20) | copy-start | bytes 1540
  106.5 119.7 %copy-start.12 = (f32[128]{0:T(128)S(1)}, f32[128]{0:T(128)}, u32[]{:S(2)}) copy-start(f32[128]{0:T(128)} %param.21) | copy-start | bytes 1540
  106.5 167.0 %all-reduce.3.cloned.1.call-start = ((), (), s32[]{:S(2)}) async-start(), calls=%async_computation.5 | async-start | bytes 131072 | tf_op jit(solution)/shard_map/psum | solution.py:62
  225.8 138.7 %reduce-scatter.5.cloned.1.call-start = ((), (), s32[]{:S(2)}) async-start(), calls=%async_computation.4 | async-start | bytes 5242880 | tf_op jit(solution)/shard_map/reduce_scatter | solution.py:76
  275.9 88.6 %copy-start.10 = (bf16[128,128]{1,0:T(8,128)(2,1)S(1)}, bf16[128,128]{1,0:T(8,128)(2,1)}, u32[]{:S(2)}) copy-start(bf16[128,128]{1,0:T(8,128)(2,1)} %param.23) | copy-start | bytes 98308
Sparse Core Ops, SparseCore 0:
  42.9 53.2 all-gather.1
  106.6 115.0 reduce-scatter.2
  226.0 47.4 all-reduce.2
  279.4 85.1 reduce-scatter.4
where the time goes:
time: 375 us
  waiting for transfers between devices  301 us (80%)
  other arithmetic  40.5 us (11%)
  matrix products  17 us (5%)
  between operations  13.3 us (4%)
    reduce_scatter x1, waiting for transfers between devices, on_device(): lax.psum_scatter(jnp.einsum('hik,hjk->jhi', left, right_all, preferred_el...  115 us
    reduce_scatter x1, waiting for transfers between devices, on_device(): lax.psum_scatter(jnp.einsum('jhi,hd->jid', hidden, weight_rows, preferred...  85.3 us
    all_gather x1, waiting for transfers between devices, on_device(): right_all = lax.all_gather(right, 'row', axis=1, tiled=True)  53.4 us
    psum x1, waiting for transfers between devices, on_device(): lax.psum(second_sums.astype(jnp.bfloat16), 'chan').astype(jnp.float32)  47.2 us
    reduce_sum x1, other arithmetic, on_device(): spread = jnp.mean(shifted * shifted, axis=-1, keepdims=True)  11.6 us
    reduce_sum x1, other arithmetic, on_device(): centre = jnp.mean(source, axis=-1, keepdims=True)  10.7 us
    dot_general x1, matrix products, on_device(): jnp.einsum('hik,hjk->jhi', left, right_all, preferred_element_type=jnp.fl...  10.3 us
    convert_element_type x1, other arithmetic, on_device(): (shifted * lax.rsqrt(spread + 1e-05) * ln_gain + ln_bias).astype(jnp.bflo...  9.28 us
  transfers between devices with their start and end apart: 4, of which 4 were waited for; matrix products, arithmetic and copies ran while one was open for 0% of the time, Pallas kernels for 0%

commit v1 on v0

--- a/solution.py
+++ b/solution.py
@@ -59,7 +59,9 @@
     second_sums = jnp.sum(widened * widened, axis=1)
     first_sums, second_sums = (
         lax.psum(first_sums.astype(jnp.bfloat16), "chan").astype(jnp.float32),
-        lax.psum(second_sums.astype(jnp.bfloat16), "chan").astype(jnp.float32),
+        jnp.sum(lax.all_gather(second_sums.astype(jnp.bfloat16), "chan"), axis=0).astype(
+            jnp.float32
+        ),
     )
     total_width = group_width * lax.axis_size("chan")
     mean_hid = first_sums / total_width

time: 375 us -> 356 us (0.949)
  waiting for transfers between devices: 301 us -> 256 us
  blocking collectives: 0 us -> 28 us
    psum x1 -> x0, waiting for transfers between devices: 47.2 us -> none  [on_device(): lax.psum(second_sums.astype(jnp.bfloat16), 'chan').astype(jnp.float32)]
    psum x0 -> x1, blocking collectives: none -> 14.7 us  [on_device(): lax.psum(first_sums.astype(jnp.bfloat16), 'chan').astype(jnp.float32)]
    all_gather x0 -> x1, blocking collectives: none -> 13.3 us  [on_device(): lax.all_gather(second_sums.astype(jnp.bfloat16), 'chan')]
  transfers between devices with their start and end apart: 4 -> 3, of which waited for: 4 -> 3; matrix products, arithmetic and copies ran while one was open for 0% -> 0% of each run, Pallas kernels for 0% -> 0%
where the time goes in v1:
time: 356 us
  waiting for transfers between devices  256 us (72%)
  other arithmetic  38.5 us (11%)
  blocking collectives  28 us (8%)
  matrix products  17 us (5%)
  between operations  13.3 us (4%)
    reduce_scatter x1, waiting for transfers between devices, on_device(): lax.psum_scatter(jnp.einsum('hik,hjk->jhi', left, right_all, preferred_el...  114 us
    reduce_scatter x1, waiting for transfers between devices, on_device(): lax.psum_scatter(jnp.einsum('jhi,hd->jid', hidden, weight_rows, preferred...  87.8 us
    all_gather x1, waiting for transfers between devices, on_device(): right_all = lax.all_gather(right, 'row', axis=1, tiled=True)  53.4 us
    psum x1, blocking collectives, on_device(): lax.psum(first_sums.astype(jnp.bfloat16), 'chan').astype(jnp.float32)  14.7 us
    all_gather x1, blocking collectives, on_device(): lax.all_gather(second_sums.astype(jnp.bfloat16), 'chan')  13.3 us
    reduce_sum x1, other arithmetic, on_device(): spread = jnp.mean(shifted * shifted, axis=-1, keepdims=True)  11.6 us
    reduce_sum x1, other arithmetic, on_device(): centre = jnp.mean(source, axis=-1, keepdims=True)  10.7 us
    dot_general x1, matrix products, on_device(): jnp.einsum('hik,hjk->jhi', left, right_all, preferred_element_type=jnp.fl...  10.3 us
  transfers between devices with their start and end apart: 3, of which 3 were waited for; matrix products, arithmetic and copies ran while one was open for 0% of the time, Pallas kernels for 0%

profile of v1, /device:TPU:1, one launch (start us, length us, event | category | flops | bytes accessed | tf_op | source)
XLA Modules:
  0.0 355.8 jit_solution(4830547148209230650)
XLA Ops:
  6.5 0.0 all-gather.3.cloned.1.call-start
  6.6 10.7 %convert_reduce_fusion = f32[256,64]{0,1:T(8,128)S(1)} fusion(bf16[256,64,128]{2,1,0:T(8,128)(2,1)} %param.12), kind=kLoop, calls=%fused_computation.2 | loop fusion | flops 4177920 | bytes 4259840 | tf_op jit(solution)/shard_map/reduce_sum | solution.py:26
  17.3 11.6 %fusion.2 = f32[256,64]{0,1:T(8,128)S(1)} fusion(f32[256,64]{0,1:T(8,128)S(1)} %broadcast_multiply_fusion, bf16[256,64,128]{2,1,0:T(8,128)(2,1)S(1)} %copy-done.1), kind=kLoop, calls=%fused_computation.5 | loop fusion | flops 8372224 | bytes 4325376 | tf_op jit(solution)/shard_map/reduce_sum | solution.py:28
  29.0 0.0 copy-start.4
  29.0 0.0 copy-start.5
  29.0 0.0 copy-start.6
  29.1 0.0 copy-start.7
  29.1 9.3 %fusion.5 = bf16[256,64,128]{2,0,1:T(8,128)(2,1)S(1)} fusion(f32[128]{0:T(128)S(1)} %copy-done.8, f32[128]{0:T(128)S(1)} %copy-done.9, f32[256,64]{0,1:T(8,128)S(1)} %add_rsqrt_fusion.1, f32[256,64]{0,1:T(8,128)S(1)} %broadcast_multiply_fusion, bf16[256,64,128]{2,1,0:T(8,128)(2,1)S(1)} %copy-done.1), kind=kLoop, calls=%fused_computation.8 | loop fusion | flops 12582912 | bytes 8520704 | tf_op jit(solution)/shard_map/convert_element_type | solution.py:29
  38.4 1.3 fusion.26
  39.7 0.7 copy-done.2
  40.3 2.4 fusion.13
  42.7 0.0 all-gather.3.cloned.1.call-update
  42.8 0.0 reduce-scatter.3.cloned.1.call-start
  42.8 53.4 %all-gather.3.cloned.1.call-done = bf16[32,1024,64]{1,0,2:T(8,128)(2,1)} async-done(((bf16[32,256,64]{1,0,2:T(8,128)(2,1)}), bf16[32,1024,64]{1,0,2:T(8,128)(2,1)}) %all-gather.3.cloned.1.call-update) | async-done | bytes 4194320 | tf_op jit(solution)/shard_map/all_gather | solution.py:47
  96.2 10.3 %convert_bitcast_fusion = bf16[1024,32,256]{2,0,1:T(8,128)(2,1)} fusion(bf16[32,1024,64]{1,0,2:T(8,128)(2,1)} %all-gather.3.cloned.1.call-done, bf16[32,256,64]{1,0,2:T(8,128)(2,1)S(1)} %get-tuple-element.5), kind=kOutput, calls=%fused_computation | convolution fusion | flops 1082130432 | bytes 22020096 | tf_op jit(solution)/shard_map/hik,hjk->jhi/dot_general | solution.py:49
  106.5 0.0 reduce-scatter.3.cloned.1.call-update
  106.5 0.0 reduce-scatter.5.cloned.1.call-start
  106.5 0.6 copy-done.11
  107.1 0.1 dynamic_slice.13
  107.2 0.1 dynamic_slice.14
  107.3 114.5 %reduce-scatter.3.cloned.1.call-done = bf16[64,32,256]{2,0,1:T(8,128)(2,1)} async-done(((bf16[1024,32,256]{2,0,1:T(8,128)(2,1)}), bf16[64,32,256]{2,0,1:T(8,128)(2,1)}) %reduce-scatter.3.cloned.1.call-update) | async-done | bytes 1048592 | tf_op jit(solution)/shard_map/reduce_scatter | solution.py:48
  221.7 1.4 fusion.11
  223.2 13.3 %all-gather = bf16[256,256]{1,0:T(8,128)(2,1)S(1)} all-gather(bf16[64,256]{1,0:T(8,128)(2,1)S(1)} %fusion.11), channel_id=2, replica_groups=mesh['row'=4,'col'=16,'chan'=4] {'chan'}, dimensions={0}, use_global_device_ids=true | all-gather | bytes 163840 | tf_op jit(solution)/shard_map/all_gather | solution.py:62
  236.5 1.4 reduce_sum.53
  237.8 14.7 %psum.7 = bf16[64,256]{1,0:T(8,128)(2,1)S(1)} all-reduce(bf16[64,256]{1,0:T(8,128)(2,1)S(1)} %reduce_sum.53), channel_id=1, replica_groups=mesh['row'=4,'col'=16,'chan'=4] {'chan'}, use_global_device_ids=true, to_apply=%region_4.0 | all-reduce | flops 16384 | bytes 65536 | tf_op jit(solution)/shard_map/psum | solution.py:61
  252.6 1.6 fusion.10
  254.3 0.0 copy-start.10
  254.3 3.3 convolution_convert_fusion
  257.5 0.0 reduce-scatter.5.cloned.1.call-update
  257.6 87.8 %reduce-scatter.5.cloned.1.call-done = bf16[16,256,128]{2,1,0:T(8,128)(2,1)} async-done(((bf16[64,256,128]{2,1,0:T(8,128)(2,1)}), bf16[16,256,128]{2,1,0:T(8,128)(2,1)}) %reduce-scatter.5.cloned.1.call-update) | async-done | bytes 1048592 | tf_op jit(solution)/shard_map/reduce_scatter | solution.py:78
  345.3 2.2 fusion.22
  347.6 1.6 copy.22
  (24 shorter events, 0.1 us)
Async XLA Ops:
  6.5 247.7 %copy-start = (bf16[128,128]{1,0:T(8,128)(2,1)S(1)}, bf16[128,128]{1,0:T(8,128)(2,1)}, u32[]{:S(2)}) copy-start(bf16[128,128]{1,0:T(8,128)(2,1)} %param.22) | copy-start | bytes 98308
  6.5 22.4 %copy-start.3 = (s32[256,64]{0,1:T(8,128)S(1)}, s32[256,64]{0,1:T(8,128)}, u32[]{:S(2)}) copy-start(s32[256,64]{0,1:T(8,128)} %param.13) | copy-start | bytes 196612
  6.5 22.5 %copy-start.9 = (f32[128]{0:T(128)S(1)}, f32[128]{0:T(128)}, u32[]{:S(2)}) copy-start(f32[128]{0:T(128)} %param.14) | copy-start | bytes 1540
  6.5 22.5 %copy-start.8 = (f32[128]{0:T(128)S(1)}, f32[128]{0:T(128)}, u32[]{:S(2)}) copy-start(f32[128]{0:T(128)} %param.15) | copy-start | bytes 1540
  6.5 89.7 %all-gather.3.cloned.1.call-start = ((), (), s32[]{:S(2)}) async-start(), calls=%async_computation.2 | async-start | bytes 5242880 | tf_op jit(solution)/shard_map/all_gather | solution.py:47
  6.6 10.7 %copy-start.1 = (bf16[256,64,128]{2,1,0:T(8,128)(2,1)S(1)}, bf16[256,64,128]{2,1,0:T(8,128)(2,1)}, u32[]{:S(2)}) copy-start(bf16[256,64,128]{2,1,0:T(8,128)(2,1)} %param.12) | copy-start | bytes 12582916
  29.0 9.3 %copy-start.4 = (bf16[128,32]{0,1:T(8,128)(2,1)S(1)}, bf16[128,32]{0,1:T(8,128)(2,1)}, u32[]{:S(2)}) copy-start(bf16[128,32]{0,1:T(8,128)(2,1)} %param.19) | copy-start | bytes 24580
  29.0 9.3 %copy-start.5 = (bf16[128,32]{0,1:T(8,128)(2,1)S(1)}, bf16[128,32]{0,1:T(8,128)(2,1)}, u32[]{:S(2)}) copy-start(bf16[128,32]{0,1:T(8,128)(2,1)} %param.18) | copy-start | bytes 24580
  29.0 9.3 %copy-start.6 = (bf16[128,32]{0,1:T(8,128)(2,1)S(1)}, bf16[128,32]{0,1:T(8,128)(2,1)}, u32[]{:S(2)}) copy-start(bf16[128,32]{0,1:T(8,128)(2,1)} %param.17) | copy-start | bytes 24580
  29.1 9.3 %copy-start.7 = (bf16[128,32]{0,1:T(8,128)(2,1)S(1)}, bf16[128,32]{0,1:T(8,128)(2,1)}, u32[]{:S(2)}) copy-start(bf16[128,32]{0,1:T(8,128)(2,1)} %param.16) | copy-start | bytes 24580
  38.4 1.9 copy-start.2
  42.8 179.0 %reduce-scatter.3.cloned.1.call-start = ((), (), s32[]{:S(2)}) async-start(), calls=%async_computation.3 | async-start | bytes 17825792 | tf_op jit(solution)/shard_map/reduce_scatter | solution.py:48
  106.5 0.7 copy-start.11
  106.5 0.7 copy-start.12
  106.5 238.8 %reduce-scatter.5.cloned.1.call-start = ((), (), s32[]{:S(2)}) async-start(), calls=%async_computation.4 | async-start | bytes 5242880 | tf_op jit(solution)/shard_map/reduce_scatter | solution.py:78
  254.3 91.1 %copy-start.10 = (bf16[128,128]{1,0:T(8,128)(2,1)S(1)}, bf16[128,128]{1,0:T(8,128)(2,1)}, u32[]{:S(2)}) copy-start(bf16[128,128]{1,0:T(8,128)(2,1)} %param.23) | copy-start | bytes 98308
Sparse Core Ops, SparseCore 0:
  42.9 53.2 all-gather.2
  106.6 115.0 reduce-scatter.2
  257.7 87.5 reduce-scatter.4
